TPU v7x, 256 devices: a whole 4x4x8 slice. The times are simulated.
256 devices in a mesh: row: 32 (over x, y, core), col: 8 (over z).
Axes of the slice: x: 4, y: 4, z: 8, core: 2. Of those that a mesh axis runs over, the one named last changes fastest.
Arguments:
- solution: float32 [64, 65536], P(None, ('row', 'col')), may hold values from -6 to 6
- residual: float32 [64, 262144], P(None, ('row', 'col')), may hold values from -6 to 6
- direction: float32 [64, 65536], P(None, ('row', 'col')), may hold values from -6 to 6
- jacobian_tiles: bfloat16 [2048, 40, 128, 128], P('row', 'col'), may hold values from -0.078125 to 0.078125
- tile_blocks: int32 [2048, 40], P('row', 'col'), may hold values from 0 to 63, as said below
- tile_counts: int32 [2048, 8], P('row', 'col'), may hold values from 1 to 5, as said below
Outputs:
- solution_next: float32 [64, 65536], P(None, ('row', 'col'))
- residual_next: float32 [64, 262144], P(None, ('row', 'col'))
- direction_next: float32 [64, 65536], P(None, ('row', 'col'))
Inputs may be any that keep to these rules, and one draw needn't show every extreme that they name: `tile_blocks`: within each sensor and parameter group the 5 entries are different. Only the first tile_counts[i, c] slots of sensor i in group c hold a tile; some sensor fills all 5 slots of every group.
All inputs are finite; a program needn't handle non-finite values.
Results may differ from a plain program's by a relative error of at most 0.023.
Values may be sent and summed in bfloat16 or wider, within the bound.
A program may use at most 128 MiB of HBM per device.

v0:
```python
import functools

import jax
import jax.numpy as jnp
from jax import lax
from jax.sharding import Mesh
from jax.sharding import PartitionSpec as P

CB_DEV = 64
ITERS = 2
ROW = ("row_0", "row_1", "row_2")
ROW_COL = ("row_0", "row_1", "row_2", "col")


def in_blocks(value, dim, devices):
    before, after = (value.shape[:dim], value.shape[dim + 1 :])
    return jnp.moveaxis(value.reshape(*before, devices, -1, *after), dim, 0)


def sent_and_summed(value, axis, dim):
    devices = lax.axis_size(axis)
    tiles = lax.all_to_all(in_blocks(value, dim, devices), axis, 0, 0, tiled=True)
    return jnp.sum(tiles.astype(jnp.float32), axis=0)


def over_axes(value, axes):
    return functools.reduce(lax.psum, axes, value)


def laid_out(tiles, dim):
    tiles = jnp.moveaxis(tiles, 0, dim)
    lengths = tiles.shape
    return tiles.reshape(*lengths[:dim], lengths[dim] * lengths[dim + 1], *lengths[dim + 2 :])


def copy_for_each(value, axis):
    devices = lax.axis_size(axis)
    return lax.all_to_all(
        jnp.broadcast_to(value[None], (devices, *value.shape)), axis, 0, 0, tiled=True
    )


def collect(value, axis, dim):
    return laid_out(copy_for_each(value, axis), dim)


def times_highest(left, right):
    return jnp.dot(left, right, precision=lax.Precision.HIGHEST)


def gram_matrix(values):
    return jnp.dot(values, values.T, precision=lax.Precision.HIGHEST)


def solve_spd(matrix, right):
    factor_low = jnp.linalg.cholesky(matrix)
    middle = lax.linalg.triangular_solve(factor_low, right, left_side=True, lower=True)
    return lax.linalg.triangular_solve(
        factor_low, middle, left_side=True, lower=True, transpose_a=True
    )


def images(jacobian_tiles, tile_blocks, live_slot, direction_half):
    rhs_count = direction_half.shape[0]
    tile_width = jacobian_tiles.shape[2]
    table_view = direction_half.reshape(rhs_count, -1, tile_width)
    picked = jnp.take(table_view, tile_blocks, axis=1) * live_slot[None, :, :, None]
    product = jnp.einsum(
        "rsab,nrsb->nra", jacobian_tiles, picked, preferred_element_type=jnp.float32
    )
    return product.reshape(rhs_count, -1)


def gradients(jacobian_tiles, tile_blocks, live_slot, rows_half):
    rhs_count = rows_half.shape[0]
    tile_width = jacobian_tiles.shape[2]
    sensors = jacobian_tiles.shape[0]
    row_view = rows_half.reshape(rhs_count, sensors, tile_width)
    contrib = jnp.einsum(
        "rsab,nra->rsnb", jacobian_tiles, row_view, preferred_element_type=jnp.float32
    )
    contrib = contrib * live_slot.astype(jnp.float32)[:, :, None, None]
    summed = jax.ops.segment_sum(
        contrib.reshape(-1, rhs_count, tile_width), tile_blocks.reshape(-1), num_segments=CB_DEV
    )
    return summed.transpose(1, 0, 2).reshape(rhs_count, CB_DEV * tile_width)


def per_device(solution, residual, direction, jacobian_tiles, tile_blocks, tile_counts):
    live_slot = (
        jnp.arange(jacobian_tiles.shape[1], dtype=jnp.int32)[None, :] < tile_counts
    ).astype(jnp.bfloat16)
    share_rows = residual.shape[1]
    col_start = lax.axis_index("col") * share_rows
    rows_now = lax.all_gather(residual.astype(jnp.bfloat16), "col", axis=1, tiled=True).astype(
        residual.dtype
    )

    def gradient_step(rows_value):
        rows_half = rows_value.astype(jnp.bfloat16)
        partial_term = gradients(jacobian_tiles, tile_blocks, live_slot, rows_half)
        gradient = sent_and_summed(partial_term.astype(jnp.bfloat16), ROW, 1)
        gamma_value = over_axes(gram_matrix(gradient), ROW_COL)
        return (gradient, gamma_value)

    gradient, gamma_now = gradient_step(rows_now)
    iterate = solution
    for iteration in range(ITERS):
        direction_half = collect(direction.astype(jnp.bfloat16), ROW, 1)
        image_partial_term = images(jacobian_tiles, tile_blocks, live_slot, direction_half)
        image = lax.psum(image_partial_term.astype(jnp.bfloat16), "col").astype(jnp.float32)
        curvature = over_axes(gram_matrix(image), ROW)
        image, curvature = (image, curvature)
        step_alpha = solve_spd(curvature, gamma_now)
        iterate = iterate + times_highest(step_alpha.T, direction)
        rows_now = rows_now - times_highest(step_alpha.T, image)
        gradient, gamma_next = gradient_step(rows_now)
        step_beta = solve_spd(gamma_now, gamma_next)
        direction = gradient + times_highest(step_beta.T, direction)
        gamma_now = gamma_next
    residual_out = lax.dynamic_slice_in_dim(rows_now, col_start, share_rows, 1)
    return (iterate, residual_out, direction)


def solution(mesh):
    torus = Mesh(
        mesh.devices.reshape(4, 4, 2, mesh.shape["col"]), ("row_0", "row_1", "row_2", "col")
    )
    in_specs = (
        P(None, ROW_COL),
        P(None, ROW_COL),
        P(None, ROW_COL),
        P(ROW, "col", None, None),
        P(ROW, "col"),
        P(ROW, "col"),
    )
    out_specs = (P(None, ROW_COL), P(None, ROW_COL), P(None, ROW_COL))
    return jax.shard_map(
        per_device, mesh=torus, in_specs=in_specs, out_specs=out_specs, check_vma=False
    )
```

profile of v0, /device:TPU:4, one launch (start us, length us, event | category | flops | bytes accessed | tf_op | source)
XLA Modules:
  0.0 678.9 jit_solution(5240777342642542572)
XLA Ops:
  33.3 13.3 %gather_fusion = bf16[320,64,128]{2,1,0:T(8,128)(2,1)} fusion(bf16[64,64,128]{2,0,1:T(8,128)(2,1)S(1)} %copy.70, s32[1024]{0:T(1024)S(1)} %pad_clamp_fusion), kind=kCustom, calls=%fused_computation.clone | custom fusion | bytes 10487040 | tf_op jit(solution)/shard_map/jit(_take)/gather | solution.py:67
  46.6 10.1 %fusion.10 = bf16[64,8,8,128]{3,2,1,0:T(8,128)(2,1)S(1)} fusion(bf16[64,5,128,128]{3,2,1,0:T(8,128)(2,1)} %param.16, bf16[64,5,64,128]{3,2,1,0:T(8,128)(2,1)} %bitcast.164, pred[64,5]{1,0:T(8,128)(4,1)S(1)} %copy.67, bf16[64,5]{1,0:T(8,128)(2,1)S(1)} %get-tuple-element.13), kind=kOutput, calls=%fused_computation.27 | convolution fusion | flops 676855808 | bytes 16778176 | tf_op jit(solution)/shard_map/rsab,nrsb->nra/dot_general | solution.py:68
  62.9 10.2 %broadcast_multiply_fusion.2 = f32[64,64,5,128]{3,1,2,0:T(8,128)} fusion(f32[64,5]{1,0:T(8,128)S(1)} %get-tuple-element.14, bf16[64,5,128,128]{3,2,1,0:T(8,128)(2,1)} %param.16, bf16[64,64,128,1]{2,1,0,3:T(8,128)(2,1)S(1)} %bitcast.166), kind=kOutput, calls=%fused_computation.15 | convolution fusion | flops 673710080 | bytes 22021376 | tf_op jit(solution)/shard_map/rsab,nra->rsnb/dot_general | solution.py:79
  73.3 33.3 %scatter_fusion = f32[64,64,128]{2,1,0:T(8,128)S(1)} fusion(f32[64,64,128]{2,1,0:T(8,128)S(1)} %broadcast.78.clone, s32[320]{0:T(512)S(1)} %reshape.148, f32[320,64,128]{2,1,0:T(8,128)} %bitcast.161), kind=kCustom, calls=%fused_computation.2 | custom fusion | flops 2621440 | bytes 31458560 | tf_op jit(solution)/shard_map/scatter-add | solution.py:83
  116.9 21.1 %all-reduce.6.cloned.1.call-done = bf16[64,8192]{1,0:T(8,128)(2,1)} async-done(((bf16[64,8192]{1,0:T(8,128)(2,1)}), bf16[64,8192]{1,0:T(8,128)(2,1)}) %all-reduce.6.cloned.1.call-update) | async-done | bytes 1048592 | tf_op jit(solution)/shard_map/psum | solution.py:111
  140.3 16.0 %all-reduce.1 = (f32[64,64]{0,1:T(8,128)S(1)}, f32[64,64]{0,1:T(8,128)S(1)}) all-reduce(f32[64,64]{0,1:T(8,128)S(1)} %fusion.45, f32[64,64]{0,1:T(8,128)S(1)} %fusion.44), channel_id=1, replica_groups=mesh['row_0'=4,'row_1'=4,'row_2'=2,'col'=8] {'row_0'}, use_global_device_ids=true, to_apply=%region_8.0 | all-reduce | flops 8192 | bytes 65536 | tf_op jit(solution)/shard_map/psum | solution.py:27
  156.3 17.6 %all-reduce = (f32[64,64]{0,1:T(8,128)S(1)}, f32[64,64]{0,1:T(8,128)S(1)}) all-reduce(f32[64,64]{0,1:T(8,128)S(1)} %get-tuple-element.9, f32[64,64]{0,1:T(8,128)S(1)} %get-tuple-element.10), channel_id=1, replica_groups=mesh['row_0'=4,'row_1'=4,'row_2'=2,'col'=8] {'row_1'}, use_global_device_ids=true, to_apply=%region_9.0 | all-reduce | flops 8192 | bytes 65536 | tf_op jit(solution)/shard_map/psum | solution.py:27
  177.5 29.1 %psum.147 = f32[64,64]{0,1:T(8,128)S(1)} all-reduce(f32[64,64]{0,1:T(8,128)S(1)} %get-tuple-element.11), channel_id=1, replica_groups=mesh['row_0'=4,'row_1'=4,'row_2'=2,'col'=8] {'col'}, use_global_device_ids=true, to_apply=%region_11.14 | all-reduce | flops 4096 | bytes 32768 | tf_op jit(solution)/shard_map/psum | solution.py:27
  223.3 10.2 %broadcast_multiply_fusion.1 = f32[64,64,5,128]{3,1,2,0:T(8,128)} fusion(f32[64,5]{1,0:T(8,128)S(1)} %get-tuple-element.14, bf16[64,5,128,128]{3,2,1,0:T(8,128)(2,1)} %param.16, bf16[64,64,128,1]{2,1,0,3:T(8,128)(2,1)S(1)} %bitcast.167), kind=kOutput, calls=%fused_computation.14 | convolution fusion | flops 673710080 | bytes 22021376 | tf_op jit(solution)/shard_map/rsab,nra->rsnb/dot_general | solution.py:79
  233.7 33.0 %scatter_fusion.1 = f32[64,64,128]{2,1,0:T(8,128)S(1)} fusion(f32[64,64,128]{2,1,0:T(8,128)S(1)} %broadcast.78.clone.1, s32[320]{0:T(512)S(1)} %reshape.148, f32[320,64,128]{2,1,0:T(8,128)} %bitcast.162), kind=kCustom, calls=%fused_computation.3 | custom fusion | flops 2621440 | bytes 31458560 | tf_op jit(solution)/shard_map/scatter-add | solution.py:83
  269.6 16.1 %all-to-all-start.2 = ((bf16[32,64,256]{2,1,0:T(8,128)(2,1)}), bf16[32,64,256]{2,1,0:T(8,128)(2,1)S(1)}, u32[]{:S(2)}, u32[]{:S(2)}) async-start(bf16[32,64,256]{2,1,0:T(8,128)(2,1)} %copy.82), calls=%async_computation.2 | async-start | bytes 2097152 | tf_op jit(solution)/shard_map/all_to_all | solution.py:22
  300.8 16.0 %psum.148 = f32[64,64]{0,1:T(8,128)S(1)} all-reduce(f32[64,64]{0,1:T(8,128)S(1)} %fusion.46), channel_id=1, replica_groups=mesh['row_0'=4,'row_1'=4,'row_2'=2,'col'=8] {'row_0'}, use_global_device_ids=true, to_apply=%region_14.19 | all-reduce | flops 4096 | bytes 32768 | tf_op jit(solution)/shard_map/psum | solution.py:27
  316.8 15.4 %psum.149 = f32[64,64]{0,1:T(8,128)S(1)} all-reduce(f32[64,64]{0,1:T(8,128)S(1)} %psum.148), channel_id=1, replica_groups=mesh['row_0'=4,'row_1'=4,'row_2'=2,'col'=8] {'row_1'}, use_global_device_ids=true, to_apply=%region_15.20 | all-reduce | flops 4096 | bytes 32768 | tf_op jit(solution)/shard_map/psum | solution.py:27
  335.7 27.1 %psum.151 = f32[64,64]{0,1:T(8,128)S(1)} all-reduce(f32[64,64]{0,1:T(8,128)S(1)} %psum.150), channel_id=1, replica_groups=mesh['row_0'=4,'row_1'=4,'row_2'=2,'col'=8] {'col'}, use_global_device_ids=true, to_apply=%region_17.22 | all-reduce | flops 4096 | bytes 32768 | tf_op jit(solution)/shard_map/psum | solution.py:27
  363.6 20.5 %all_to_all.25 = bf16[32,64,256]{2,1,0:T(8,128)(2,1)S(1)} all-to-all(bf16[32,64,256]{2,1,0:T(8,128)(2,1)S(1)} %broadcast_in_dim.15), channel_id=1, replica_groups=mesh['row_0'=4,'row_1'=4,'row_2'=2,'col'=8] {'row_0','row_1','row_2'}, dimensions={0} | all-to-all | bytes 2097152 | tf_op jit(solution)/shard_map/all_to_all | solution.py:38
  385.7 13.3 %gather_fusion.1 = bf16[320,64,128]{2,1,0:T(8,128)(2,1)} fusion(bf16[64,64,128]{2,0,1:T(8,128)(2,1)S(1)} %copy.87, s32[1024]{0:T(1024)S(1)} %pad_clamp_fusion), kind=kCustom, calls=%fused_computation.1.clone | custom fusion | bytes 10487040 | tf_op jit(solution)/shard_map/jit(_take)/gather | solution.py:67
  410.8 72.9 %all-reduce.8.cloned.1.call-done = bf16[64,8192]{1,0:T(8,128)(2,1)} async-done(((bf16[64,8192]{1,0:T(8,128)(2,1)}), bf16[64,8192]{1,0:T(8,128)(2,1)}) %all-reduce.8.cloned.1.call-update) | async-done | bytes 1048592 | tf_op jit(solution)/shard_map/psum | solution.py:111
  485.6 15.5 %psum.153 = f32[64,64]{0,1:T(8,128)S(1)} all-reduce(f32[64,64]{0,1:T(8,128)S(1)} %fusion.47), channel_id=1, replica_groups=mesh['row_0'=4,'row_1'=4,'row_2'=2,'col'=8] {'row_0'}, use_global_device_ids=true, to_apply=%region_19.24 | all-reduce | flops 4096 | bytes 32768 | tf_op jit(solution)/shard_map/psum | solution.py:27
  501.1 17.0 %psum.154 = f32[64,64]{0,1:T(8,128)S(1)} all-reduce(f32[64,64]{0,1:T(8,128)S(1)} %psum.153), channel_id=1, replica_groups=mesh['row_0'=4,'row_1'=4,'row_2'=2,'col'=8] {'row_1'}, use_global_device_ids=true, to_apply=%region_20.25 | all-reduce | flops 4096 | bytes 32768 | tf_op jit(solution)/shard_map/psum | solution.py:27
  538.4 10.2 %broadcast_multiply_fusion = f32[64,64,5,128]{3,1,2,0:T(8,128)} fusion(f32[64,5]{1,0:T(8,128)S(1)} %get-tuple-element.14, bf16[64,5,128,128]{3,2,1,0:T(8,128)(2,1)} %param.16, bf16[64,64,128,1]{2,1,0,3:T(8,128)(2,1)S(1)} %bitcast.165), kind=kOutput, calls=%fused_computation.13 | convolution fusion | flops 673710080 | bytes 22021376 | tf_op jit(solution)/shard_map/rsab,nra->rsnb/dot_general | solution.py:79
  548.8 33.0 %scatter_fusion.2 = f32[64,64,128]{2,1,0:T(8,128)S(1)} fusion(f32[64,64,128]{2,1,0:T(8,128)S(1)} %broadcast.78, s32[320]{0:T(512)S(1)} %reshape.148, f32[320,64,128]{2,1,0:T(8,128)} %bitcast.160), kind=kCustom, calls=%fused_computation.4 | custom fusion | flops 2621440 | bytes 31458560 | tf_op jit(solution)/shard_map/scatter-add | solution.py:83
  605.8 15.9 %psum.156 = f32[64,64]{1,0:T(8,128)S(1)} all-reduce(f32[64,64]{1,0:T(8,128)S(1)} %fusion.48), channel_id=1, replica_groups=mesh['row_0'=4,'row_1'=4,'row_2'=2,'col'=8] {'row_0'}, use_global_device_ids=true, to_apply=%region_24.29 | all-reduce | flops 4096 | bytes 32768 | tf_op jit(solution)/shard_map/psum | solution.py:27
  621.7 16.4 %psum.157 = f32[64,64]{1,0:T(8,128)S(1)} all-reduce(f32[64,64]{1,0:T(8,128)S(1)} %psum.156), channel_id=1, replica_groups=mesh['row_0'=4,'row_1'=4,'row_2'=2,'col'=8] {'row_1'}, use_global_device_ids=true, to_apply=%region_25.30 | all-reduce | flops 4096 | bytes 32768 | tf_op jit(solution)/shard_map/psum | solution.py:27
  641.5 29.1 %psum.159 = f32[64,64]{1,0:T(8,128)S(1)} all-reduce(f32[64,64]{1,0:T(8,128)S(1)} %psum.158), channel_id=1, replica_groups=mesh['row_0'=4,'row_1'=4,'row_2'=2,'col'=8] {'col'}, use_global_device_ids=true, to_apply=%region_27.32 | all-reduce | flops 4096 | bytes 32768 | tf_op jit(solution)/shard_map/psum | solution.py:27
  (123 shorter events, 151.8 us)
Async XLA Ops:
  9.1 22.5 %all-to-all-start = ((bf16[32,64,256]{2,1,0:T(8,128)(2,1)}), bf16[32,64,256]{2,1,0:T(8,128)(2,1)S(1)}, u32[]{:S(2)}, u32[]{:S(2)}) async-start(bf16[32,64,256]{2,1,0:T(8,128)(2,1)} %broadcast_in_dim.13), calls=%async_computation | async-start | bytes 2097152 | tf_op jit(solution)/shard_map/all_to_all | solution.py:38
  16.7 44.7 %all-gather.2.cloned.1.call-start = ((), (), s32[]{:S(2)}) async-start(), calls=%async_computation.6 | async-start | bytes 1179648 | tf_op jit(solution)/shard_map/all_gather | solution.py:95
  18.4 119.6 %all-reduce.6.cloned.1.call-start = ((), (), s32[]{:S(2)}) async-start(), calls=%async_computation.5 | async-start | bytes 2097152 | tf_op jit(solution)/shard_map/psum | solution.py:111
  107.5 111.8 %copy-start.3 = (bf16[64,8192]{1,0:T(8,128)(2,1)S(1)}, bf16[64,8192]{1,0:T(8,128)(2,1)}, u32[]{:S(2)}) copy-start(bf16[64,8192]{1,0:T(8,128)(2,1)} %all-gather.2.cloned.1.call-done) | copy-start | bytes 3145732
  109.5 30.5 %all-to-all-start.1 = ((bf16[32,64,256]{2,1,0:T(8,128)(2,1)}), bf16[32,64,256]{2,1,0:T(8,128)(2,1)S(1)}, u32[]{:S(2)}, u32[]{:S(2)}) async-start(bf16[32,64,256]{2,1,0:T(8,128)(2,1)} %copy.77), calls=%async_computation.1 | async-start | bytes 2097152 | tf_op jit(solution)/shard_map/all_to_all | solution.py:22
  221.6 1.3 copy-start
  266.9 96.3 %copy-start.4 = (f32[64,256]{1,0:T(8,128)S(1)}, f32[64,256]{1,0:T(8,128)}, u32[]{:S(2)}) copy-start(f32[64,256]{1,0:T(8,128)} %param.15) | copy-start | bytes 196612
  269.6 30.8 %all-to-all-start.2 = ((bf16[32,64,256]{2,1,0:T(8,128)(2,1)}), bf16[32,64,256]{2,1,0:T(8,128)(2,1)S(1)}, u32[]{:S(2)}, u32[]{:S(2)}) async-start(bf16[32,64,256]{2,1,0:T(8,128)(2,1)} %copy.82), calls=%async_computation.2 | async-start | bytes 2097152 | tf_op jit(solution)/shard_map/all_to_all | solution.py:22
  285.7 197.9 %all-reduce.8.cloned.1.call-start = ((), (), s32[]{:S(2)}) async-start(), calls=%async_computation.7 | async-start | bytes 2097152 | tf_op jit(solution)/shard_map/psum | solution.py:111
  399.1 11.3 %copy-start.5 = (f32[64,256]{1,0:T(8,128)S(1)}, f32[64,256]{1,0:T(8,128)}, u32[]{:S(2)}) copy-start(f32[64,256]{1,0:T(8,128)} %param.13) | copy-start | bytes 196612
  409.1 125.2 %copy-start.1 = (f32[64,8192]{1,0:T(8,128)S(1)}, f32[64,8192]{1,0:T(8,128)}, u32[]{:S(2)}) copy-start(f32[64,8192]{1,0:T(8,128)} %copy-done) | copy-start | bytes 6291460
  536.7 1.3 copy-start.2
  584.7 20.7 %all-to-all-start.4 = ((bf16[32,64,256]{2,1,0:T(8,128)(2,1)}), bf16[32,64,256]{2,1,0:T(8,128)(2,1)S(1)}, u32[]{:S(2)}, u32[]{:S(2)}) async-start(bf16[32,64,256]{2,1,0:T(8,128)(2,1)} %copy.93), calls=%async_computation.4 | async-start | bytes 2097152 | tf_op jit(solution)/shard_map/all_to_all | solution.py:22
Sparse Core Ops, SparseCore 0:
  19.9 41.4 all-gather.1
  63.8 74.2 all-reduce.5
  410.5 73.0 all-reduce.7
where the time goes:
time: 692 us; the launch traced here: 679 us
  blocking collectives  250 us (36%)
  other arithmetic  154 us (22%)
  waiting for transfers between devices  110 us (16%)
  matrix products  63.6 us (9%)
  local copies, waits for them, and re-layouts  50.2 us (7%)
  starting transfers between devices  37.1 us (5%)
  between operations  14.8 us (2%)
    psum x15, blocking collectives, over_axes(): return functools.reduce(lax.psum, axes, value)  229 us
    scatter-add x3, other arithmetic, gradients(): jax.ops.segment_sum(contrib.reshape(-1, rhs_count, tile_width), tile_bloc...  99.3 us
    psum x2, waiting for transfers between devices, per_device(): lax.psum(image_partial_term.astype(jnp.bfloat16), 'col').astype(jnp.float32)  94 us
    dot_general x3, matrix products, gradients(): jnp.einsum('rsab,nra->rsnb', jacobian_tiles, row_view, preferred_element_...  30.5 us
    all_to_all x3, starting transfers between devices, sent_and_summed(): lax.all_to_all(in_blocks(value, dim, devices), axis, 0, 0, tiled=True)  29.3 us
    gather x2, local copies, waits for them, and re-layouts, images(): jnp.take(table_view, tile_blocks, axis=1) * live_slot[None, :, :, None]  26.7 us
    another operation x12, other arithmetic, solve_spd(): factor_low = jnp.linalg.cholesky(matrix)  26.1 us
    another operation x8, other arithmetic, solve_spd(): lax.linalg.triangular_solve(factor_low, middle, left_side=True, lower=Tru...  22.2 us
  transfers between devices with their start and end apart: 7, of which 6 were waited for; matrix products, arithmetic and copies ran while one was open for 16% of the time, Pallas kernels for 0%

commit v1 on v0

v1 whole, which is shorter than its diff:
```python
import functools

import jax
import jax.numpy as jnp
from jax import lax
from jax.experimental import pallas as pl
from jax.experimental.pallas import tpu as pltpu
from jax.sharding import PartitionSpec as P

MESH = pl.DeviceIdType.MESH
F32, BF16 = jnp.float32, jnp.bfloat16
TB = 128
HOPS = 4
HIGH = lax.Precision.HIGHEST


def dot_high(left, right):
    return jnp.dot(left, right, precision=HIGH, preferred_element_type=F32)


def dot_lanes(left, right, precision=None):
    return lax.dot_general(
        left, right, (((1,), (1,)), ((), ())), precision=precision, preferred_element_type=F32
    )


def gram(value):
    return dot_lanes(value, value, HIGH)


def side_by_side(parts):
    return jnp.concatenate(parts, axis=1)


def inverses(matrices):
    size = matrices[0].shape[0]
    rows = lax.broadcasted_iota(jnp.int32, (size, 2 * size), 0)
    lanes = lax.broadcasted_iota(jnp.int32, (size, 2 * size), 1)
    eye = jnp.where(rows + size == lanes, 1.0, 0.0).astype(F32)[:, size:]

    def step(k, works):
        done = []
        for work in works:
            row = jnp.sum(jnp.where(rows == k, work, 0.0), axis=0, keepdims=True)
            col = jnp.sum(jnp.where(lanes == k, work, 0.0), axis=1, keepdims=True)
            pivot = jnp.sum(jnp.where(lanes[:1] == k, row, 0.0), axis=1, keepdims=True)
            row = row / pivot
            done.append(jnp.where(rows == k, row, work - col * row))
        return tuple(done)

    works = lax.fori_loop(0, size, step, tuple(side_by_side([a, eye]) for a in matrices))
    return [work[:, size:] for work in works]


class Ring:
    @staticmethod
    def exists(d, t, h):
        return 1 <= t <= HOPS and (t < HOPS or h == d)


def kernel(
    ny,
    slots,
    gidx,
    perm,
    keep,
    last,
    has,
    sol_ref,
    res_ref,
    dir_ref,
    tiles_hbm,
    sol_out,
    res_out,
    dir_out,
    tiles,
    contrib,
    prefix,
    dirbuf,
    gbuf,
    rowsbuf,
    imgbuf,
    part,
    ringout,
    ringland,
    imgshare,
    xout,
    xland,
    sbuf,
    rland,
    gshare,
    hshare,
    dnext,
    ar_in,
    ar_z,
    ar_c,
    ar_x,
    ar_out,
    tile_sem,
    ring_send,
    ring_recv,
    agr_send,
    agr_recv,
    fwd_send,
    fwd_recv,
    x_send,
    x_recv,
    rs_send,
    rs_recv,
    ar_send,
    ar_recv,
):
    rows, cols = lax.axis_size("row"), lax.axis_size("col")
    chips = rows // 2
    nx = chips // ny
    r, z = lax.axis_index("row"), lax.axis_index("col")
    core, chip = lax.rem(r, 2), r // 2
    cx, cy = chip // ny, lax.rem(chip, ny)
    share = res_ref.shape[1] // TB
    half = share // 2
    blocks = 2 * rows
    hb = blocks // 2
    group = 2 * ny
    rhs = res_ref.shape[0]

    def at_col(d):
        return lax.rem(z + d + cols, cols)

    def ring_dev(d):
        return (r, at_col(1 if d == 0 else -1))

    sibling = (r + 1 - 2 * core, z)

    def chip_at(dx, dy):
        return lax.rem(cx + dx, nx) * ny + lax.rem(cy + dy, ny)

    offsets = [(dx, dy) for dx in range(nx) for dy in range(ny)]
    others = sorted(
        offsets[1:], key=lambda o: (-(min(o[0], nx - o[0]) + min(o[1], ny - o[1])), o)
    )

    def remote(src, dst, ss, rs, dev):
        return pltpu.make_async_remote_copy(
            src_ref=src, dst_ref=dst, send_sem=ss, recv_sem=rs, device_id=dev, device_id_type=MESH
        )

    per_chunk = share * slots
    chunk_copies = []
    for c in range(cols):
        cc = at_col(cols // 2 + c) if False else c
        chunk_copies.append(
            pltpu.make_async_copy(
                tiles_hbm.at[pl.ds(cc * per_chunk, per_chunk)],
                tiles.at[pl.ds(cc * per_chunk, per_chunk)],
                tile_sem.at[c],
            )
        )
        chunk_copies[-1].start()

    mine = core * hb + 2 * chip
    for j in range(2):
        dirbuf[mine + j] = dir_ref[:, j * TB : (j + 1) * TB].astype(BF16)
    dirbuf[blocks] = jnp.zeros((rhs, TB), BF16)
    gbuf[blocks] = jnp.zeros((rhs, TB), BF16)
    for i in range(share):
        rowsbuf[z * share + i] = res_ref[:, i * TB : (i + 1) * TB].astype(BF16)

    barrier = pltpu.get_barrier_semaphore()
    partners = [sibling]
    partners += [(chip_at(*o) * 2 + core, z) for o in others]
    partners += [(r, at_col(d)) for d in range(1, cols)]
    for dev in partners:
        pl.semaphore_signal(barrier, inc=1, device_id=dev, device_id_type=MESH)
    pl.semaphore_wait(barrier, len(partners))

    def sensor_tiles(sensor):
        return side_by_side([tiles[sensor * slots + s] for s in range(slots)])

    def grad_piece(buf, shard, h):
        def one(i, _):
            sensor = shard * share + h * half + i
            value = jnp.dot(buf[sensor], sensor_tiles(sensor), preferred_element_type=F32)
            for s in range(slots):
                contrib[sensor * slots + s] = value[:, s * TB : (s + 1) * TB]
            return 0

        lax.fori_loop(0, half, one, 0, unroll=True)

    def image_piece(buf, dest, h):
        def one(i, _):
            sensor = dest * share + h * half + i
            picked = side_by_side([buf[gidx[sensor * slots + s]] for s in range(slots)])
            part[i] = dot_lanes(picked, sensor_tiles(sensor))
            return 0

        lax.fori_loop(0, half, one, 0, unroll=True)

    def sorted_sums():
        def one(j, run):
            run = run * keep[j] + contrib[perm[j]]
            prefix[j] = run
            return run

        lax.fori_loop(0, contrib.shape[0], one, jnp.zeros((rhs, TB), F32), unroll=4)

    def block_sum(k):
        return prefix[last[k]] * has[k]

    def ring_gather(buf, ss, rs):
        def piece(d, t, h):
            step = (t - 1) if d == 0 else (1 - t)
            return buf.at[pl.ds(at_col(-step) * share + h * half, half)]

        def hop(d, t, h):
            ref = piece(d, t, h)
            return remote(ref, ref, ss.at[d, t - 1, h], rs.at[d, t - 1, h], ring_dev(d))

        def landed(d, t, h):
            ref = piece(d, t + 1, h)
            return remote(ref, ref, ss.at[d, t - 1, h], rs.at[d, t - 1, h], ring_dev(d))

        for h in range(2):
            for d in range(2):
                hop(d, 1, h).start()
        for h in range(2):
            yield (z, h)
        for t in range(1, HOPS + 1):
            for h in range(2):
                for d in range(2):
                    if not Ring.exists(d, t, h):
                        continue
                    landed(d, t, h).wait_recv()
                    if Ring.exists(d, t + 1, h):
                        hop(d, t + 1, h).start()
                    yield (at_col(-t if d == 0 else t), h)
        for t in range(1, HOPS + 1):
            for h in range(2):
                for d in range(2):
                    if Ring.exists(d, t, h):
                        hop(d, t, h).wait_send()

    def ring_scatter(buf, land, out, ss, rs, wait_tiles):
        def hop(d, t, h):
            return remote(
                ringout.at[d, t - 1, h],
                land.at[d, t - 1, h],
                ss.at[d, t - 1, h],
                rs.at[d, t - 1, h],
                ring_dev(d),
            )

        def came(d, t, h):
            return Ring.exists(d, HOPS + 1 - t, h)

        order = []
        for t in range(1, HOPS + 1):
            for h in range(2):
                for d in range(2):
                    if came(d, t, h):
                        order.append((0 if not (t > 1 and came(d, t - 1, h)) else t, t, h, d))
        for _, t, h, d in sorted(order):
            away = HOPS + 1 - t
            dest = at_col(away if d == 0 else -away)
            image_piece(buf, dest, h)
            if t > 1 and came(d, t - 1, h):
                hop(d, t - 1, h).wait_recv()
                for i in range(half):
                    ringout[d, t - 1, h, i] = (part[i] + land[d, t - 2, h, i].astype(F32)).astype(BF16)
            else:
                for i in range(half):
                    ringout[d, t - 1, h, i] = part[i].astype(BF16)
            hop(d, t, h).start()
            yield
        for h in range(2):
            image_piece(buf, z, h)
            for d in range(2):
                hop(d, HOPS, h).wait_recv()
            for i in range(half):
                total = part[i]
                for d in range(2):
                    total = total + land[d, HOPS - 1, h, i].astype(F32)
                out[h * half + i] = total
            yield
        for t in range(1, HOPS + 1):
            for h in range(2):
                for d in range(2):
                    if came(d, t, h):
                        hop(d, t, h).wait_send()

    def plane(dx):
        return lax.rem(cx + dx, nx)

    def row_gather(buf, n):
        own = buf.at[pl.ds(mine, 2)]
        for dx, dy in others:
            remote(
                own,
                own,
                agr_send.at[n],
                agr_recv.at[n, (nx - dx) % nx],
                (chip_at(dx, dy) * 2 + core, z),
            ).start()

        def forward(dx, side):
            ref = buf.at[pl.ds(side * hb + plane(dx) * group, group)]
            return remote(ref, ref, fwd_send.at[n, dx], fwd_recv.at[n, dx], sibling)

        order = sorted(range(nx), key=lambda dx: min(dx, nx - dx))
        yield
        for dx in order:
            count = group if dx else group - 2
            ref = buf.at[pl.ds(core * hb, count)]
            if count:
                remote(ref, ref, agr_send.at[n], agr_recv.at[n, dx], sibling).wait_recv()
            forward(dx, core).start()
            yield
        for dx in order:
            forward(dx, 1 - core).wait_recv()
        yield
        for dx in order:
            forward(dx, core).wait_send()
        ref = buf.at[pl.ds(0, 2 * len(others))]
        remote(ref, ref, agr_send.at[n], agr_recv.at[n, 0], sibling).wait_send()

    def row_scatter(n, out):
        def swap(u):
            return remote(
                xout.at[pl.ds(u * group, group)],
                xland.at[n, pl.ds(u * group, group)],
                x_send.at[n, u],
                x_recv.at[n, u],
                sibling,
            )

        for u in range(nx):
            base = (1 - core) * hb + u * group
            for b in range(group):
                xout[u * group + b] = block_sum(base + b).astype(BF16)
            swap(u).start()
        yield
        slot = {o: i for i, o in enumerate(offsets[1:])}
        for u in range(nx):
            swap(u).wait_recv()
            base = core * hb + u * group
            for b in range(group):
                total = block_sum(base + b) + xland[n, u * group + b].astype(F32)
                sbuf[u * group + b] = total.astype(BF16)
            yield
        for o in others:
            remote(
                sbuf.at[pl.ds(2 * chip_at(*o), 2)],
                rland.at[n, pl.ds(2 * slot[o], 2)],
                rs_send.at[n],
                rs_recv.at[n],
                (chip_at(*o) * 2 + core, z),
            ).start()
        for j in range(2):
            out[j] = block_sum(mine + j) + xland[n, 2 * chip + j].astype(F32)
        yield
        every = rland.at[n]
        remote(every, every, rs_send.at[n], rs_recv.at[n], sibling).wait_recv()
        for j in range(2):
            total = out[j]
            for i in range(len(others)):
                total = total + rland[n, 2 * i + j].astype(F32)
            out[j] = total
        yield
        remote(every, every, rs_send.at[n], rs_recv.at[n], sibling).wait_send()
        for u in range(nx):
            swap(u).wait_send()

    strip = rhs // cols

    def all_sum(n, value):
        ar_in[n] = value
        for d in range(1, cols):
            peer = at_col(d)
            remote(
                ar_in.at[n, pl.ds(peer * strip, strip)],
                ar_z.at[n, pl.ds((d - 1) * strip, strip)],
                ar_send.at[n, 0],
                ar_recv.at[n, 0],
                (r, peer),
            ).start()
        yield
        ref = ar_z.at[n]
        remote(ref, ref, ar_send.at[n, 0], ar_recv.at[n, 0], sibling).wait_recv()
        total = ar_in[n, pl.ds(z * strip, strip)]
        for d in range(1, cols):
            total = total + ar_z[n, (d - 1) * strip : d * strip]
        ar_c[n, 0] = total
        swap = remote(ar_c.at[n, 0], ar_c.at[n, 1], ar_send.at[n, 1], ar_recv.at[n, 1], sibling)
        swap.start()
        yield
        swap.wait_recv()
        total = total + ar_c[n, 1]
        ar_x[n, chip] = total
        own = ar_x.at[n, chip]
        for o in others:
            remote(
                own, own, ar_send.at[n, 2], ar_recv.at[n, 2], (chip_at(*o) * 2 + core, z)
            ).start()
        yield
        ref = ar_x.at[n, pl.ds(0, len(others))]
        remote(ref, ref, ar_send.at[n, 2], ar_recv.at[n, 2], sibling).wait_recv()
        total = ar_x[n, 0]
        for i in range(1, chips):
            total = total + ar_x[n, i]
        mine_rows = ar_out.at[n, pl.ds(z * strip, strip)]
        ar_out[n, pl.ds(z * strip, strip)] = total
        for d in range(1, cols):
            remote(
                mine_rows, mine_rows, ar_send.at[n, 3], ar_recv.at[n, 3], (r, at_col(d))
            ).start()
        yield
        ref = ar_out.at[n, pl.ds(0, (cols - 1) * strip)]
        remote(ref, ref, ar_send.at[n, 3], ar_recv.at[n, 3], sibling).wait_recv()
        yield
        for s, whole in ((0, ar_z.at[n]), (2, ar_x.at[n, pl.ds(0, len(others))]), (3, ref)):
            remote(whole, whole, ar_send.at[n, s], ar_recv.at[n, s], sibling).wait_send()
        swap.wait_send()

    def advance(gen, times=1):
        for _ in range(times):
            next(gen, None)

    def finish(gen):
        for _ in gen:
            pass

    def wide(ref):
        return side_by_side([ref[i] for i in range(ref.shape[0])])

    def to_blocks(value):
        return [value[:, i * TB : (i + 1) * TB] for i in range(value.shape[1] // TB)]

    def pair(left, right):
        return side_by_side([left, right])

    resid = ring_gather(rowsbuf, ring_send.at[0], ring_recv.at[0])
    first = next(resid)
    direct = row_gather(dirbuf, 0)
    advance(direct)
    for c in chunk_copies:
        c.wait()

    def grad_next(gen, buf, times):
        for _ in range(times):
            got = next(gen, None)
            if got is not None:
                grad_piece(buf, *got)

    grad_piece(rowsbuf, *first)
    grad_next(resid, rowsbuf, 3)
    advance(direct, 2)
    grad_next(resid, rowsbuf, 2)
    advance(direct, nx - 1)
    scat = ring_scatter(dirbuf, ringland.at[0], imgshare.at[0], ring_send.at[1], ring_recv.at[1], None)
    for _ in range(8):
        advance(scat)
        grad_next(resid, rowsbuf, 2)
    finish(resid)
    sorted_sums()
    rowsc = row_scatter(0, gshare)
    advance(rowsc)
    advance(scat, 3)
    advance(rowsc, nx + 1)
    finish(scat)
    finish(direct)

    inv_prev = None
    for it in range(2):
        if it == 1:
            add = to_blocks(dot_high(beta_t, wide(imgshare.at[0])))
            for i in range(share):
                imgshare[1, i] = imgshare[1, i] + add[i]
        for i in range(share):
            imgbuf[it, z * share + i] = imgshare[it, i].astype(BF16)
        gather = ring_gather(imgbuf.at[it], ring_send.at[2 + 2 * it], ring_recv.at[2 + 2 * it])
        first = next(gather)
        if it == 0:
            finish(rowsc)
            gamma_part = gram(wide(gshare))
        else:
            gamma_part = jnp.zeros((rhs, rhs), F32)
        summed = all_sum(it, pair(gram(wide(imgshare.at[it])), gamma_part))
        advance(summed)
        grad_piece(imgbuf.at[it], *first)
        grad_next(gather, imgbuf.at[it], 3)
        advance(summed)
        grad_next(gather, imgbuf.at[it], 2)
        advance(summed)
        grad_next(gather, imgbuf.at[it], 2)
        advance(summed)
        grad_next(gather, imgbuf.at[it], 4)
        advance(summed)
        grad_next(gather, imgbuf.at[it], 4)
        finish(summed)
        finish(gather)
        both = ar_out[it]
        curvature = both[:, :rhs]
        if it == 0:
            gamma = both[:, rhs:]
        sorted_sums()
        rowsc = row_scatter(1 + it, hshare)
        advance(rowsc, nx + 2)
        inv_curv, inv_gamma = inverses([curvature, gamma])
        alpha_t = dot_high(gamma, inv_curv)
        finish(rowsc)
        step_g = to_blocks(dot_high(alpha_t, wide(hshare)))
        for j in range(2):
            gshare[j] = gshare[j] - step_g[j]
            if it == 0:
                gbuf[mine + j] = gshare[j].astype(BF16)
        if it == 0:
            direct = row_gather(gbuf, 1)
            advance(direct)
        new_gamma = gram(wide(gshare))
        summed = all_sum(2 + it, pair(new_gamma, jnp.zeros((rhs, rhs), F32)))
        advance(summed)
        old_dir = dir_ref[...] if it == 0 else wide(dnext)
        old_sol = sol_ref[...] if it == 0 else sol_out[...]
        old_res = res_ref[...] if it == 0 else res_out[...]
        sol_out[...] = old_sol + dot_high(alpha_t, old_dir)
        res_out[...] = old_res - dot_high(alpha_t, wide(imgshare.at[it]))
        if it == 0:
            advance(summed)
            advance(direct, nx + 1)
            advance(summed)
            scat = ring_scatter(
                gbuf, ringland.at[1], imgshare.at[1], ring_send.at[3], ring_recv.at[3], None
            )
            advance(scat, 4)
            advance(summed)
            advance(scat, 4)
            finish(summed)
        else:
            finish(summed)
        gamma_next = ar_out[2 + it][:, :rhs]
        beta_t = dot_high(gamma_next, inv_gamma)
        step_d = dot_high(beta_t, old_dir)
        if it == 0:
            for j, value in enumerate(to_blocks(step_d)):
                dnext[j] = gshare[j] + value
            finish(scat)
            finish(direct)
        else:
            dir_out[...] = wide(gshare) + step_d
        gamma = gamma_next


def index_tables(tile_blocks, tile_counts, blocks):
    sensors, slots = tile_blocks.shape
    live = jnp.arange(slots, dtype=jnp.int32)[None, :] < tile_counts
    k = tile_blocks
    place = (k // 4) * 2 + k % 2 + ((k // 2) % 2) * (blocks // 2)
    gidx = jnp.where(live, place, blocks).reshape(-1)
    entries = sensors * slots
    order = jnp.arange(entries, dtype=jnp.int32)
    key = gidx * entries + order
    rank = jnp.sum((key[None, :] < key[:, None]).astype(jnp.int32), axis=1)
    at = rank[None, :] == order[:, None]
    perm = jnp.sum(jnp.where(at, order[None, :], 0), axis=1)
    block_of = jnp.sum(jnp.where(at, gidx[None, :], 0), axis=1)
    same = jnp.concatenate([jnp.zeros((1,), bool), block_of[1:] == block_of[:-1]])
    every = jnp.arange(blocks, dtype=jnp.int32)
    upto = jnp.sum((gidx[None, :] <= every[:, None]).astype(jnp.int32), axis=1)
    has = jnp.any(gidx[None, :] == every[:, None], axis=1)
    return (gidx, perm, same.astype(F32), jnp.maximum(upto - 1, 0), has.astype(F32))


def per_device(solution, residual, direction, jacobian_tiles, tile_blocks, tile_counts):
    rows, cols = lax.axis_size("row"), lax.axis_size("col")
    chips = rows // 2
    ny = 4 if chips % 4 == 0 else chips
    nx = chips // ny
    rhs = residual.shape[0]
    sensors, slots = tile_blocks.shape
    entries = sensors * slots
    blocks = 2 * rows
    share = residual.shape[1] // TB
    half = share // 2
    tables = index_tables(tile_blocks, tile_counts, blocks)
    tile = (rhs, TB)
    strip = rhs // cols
    vmem = pl.BlockSpec(memory_space=pltpu.VMEM)
    smem = pl.BlockSpec(memory_space=pltpu.SMEM)
    dma = pltpu.SemaphoreType.DMA
    return pl.pallas_call(
        functools.partial(kernel, ny, slots),
        out_shape=[
            jax.ShapeDtypeStruct(solution.shape, F32),
            jax.ShapeDtypeStruct(residual.shape, F32),
            jax.ShapeDtypeStruct(direction.shape, F32),
        ],
        in_specs=[smem] * 5 + [vmem] * 3 + [pl.BlockSpec(memory_space=pl.ANY)],
        out_specs=[vmem] * 3,
        scratch_shapes=[
            pltpu.VMEM((entries, TB, TB), BF16),
            pltpu.VMEM((entries, *tile), F32),
            pltpu.VMEM((entries, *tile), F32),
            pltpu.VMEM((blocks + 1, *tile), BF16),
            pltpu.VMEM((blocks + 1, *tile), BF16),
            pltpu.VMEM((sensors, *tile), BF16),
            pltpu.VMEM((2, sensors, *tile), BF16),
            pltpu.VMEM((half, *tile), F32),
            pltpu.VMEM((2, HOPS, 2, half, *tile), BF16),
            pltpu.VMEM((2, 2, HOPS, 2, half, *tile), BF16),
            pltpu.VMEM((2, share, *tile), F32),
            pltpu.VMEM((blocks // 2, *tile), BF16),
            pltpu.VMEM((3, blocks // 2, *tile), BF16),
            pltpu.VMEM((blocks // 2, *tile), BF16),
            pltpu.VMEM((3, 2 * (chips - 1), *tile), BF16),
            pltpu.VMEM((2, *tile), F32),
            pltpu.VMEM((2, *tile), F32),
            pltpu.VMEM((2, *tile), F32),
            pltpu.VMEM((4, rhs, TB), F32),
            pltpu.VMEM((4, (cols - 1) * strip, TB), F32),
            pltpu.VMEM((4, 2, strip, TB), F32),
            pltpu.VMEM((4, chips, strip, TB), F32),
            pltpu.VMEM((4, rhs, TB), F32),
            dma((cols,)),
            dma((5, 2, HOPS, 2)),
            dma((5, 2, HOPS, 2)),
            dma((2,)),
            dma((2, nx)),
            dma((2, nx)),
            dma((2, nx)),
            dma((3, nx)),
            dma((3, nx)),
            dma((3,)),
            dma((3,)),
            dma((4, 4)),
            dma((4, 4)),
        ],
        compiler_params=pltpu.CompilerParams(
            collective_id=0, has_side_effects=True, vmem_limit_bytes=58 * 1024 * 1024
        ),
    )(*tables, solution, residual, direction, jacobian_tiles.reshape(entries, TB, TB))


def solution(mesh):
    both = P(None, ("row", "col"))
    return jax.shard_map(
        per_device,
        mesh=mesh,
        in_specs=(both, both, both, P("row", "col", None, None), P("row", "col"), P("row", "col")),
        out_specs=(both, both, both),
        check_vma=False,
    )
```

time: 692 us -> 164 us (0.24)
  the two profiles are of different devices: /device:TPU:4 before, /device:TPU:1 now
where the time goes in v1:
time: 164 us; the launch traced here: 163 us
  Pallas kernels  154 us (94%)
  local copies, waits for them, and re-layouts  4.86 us (3%)
  other arithmetic  3.83 us (2%)
    pallas_call x1, Pallas kernels, per_device(): pl.pallas_call(functools.partial(kernel, ny, slots), out_shape=[jax.Shape...  154 us
    unnamed x5, local copies, waits for them, and re-layouts  4.62 us

profile of v1, /device:TPU:1, one launch (start us, length us, event | category | flops | bytes accessed | tf_op | source)
XLA Modules:
  0.0 163.4 jit_solution(13041647360458476246)
XLA Ops:
  0.6 0.7 fusion.5
  1.3 0.1 copy.10
  1.4 0.1 reshape.32.gidx
  1.6 0.0 copy-start
  1.6 0.1 fusion
  1.7 0.5 convert_element_type.15.has
  2.2 0.1 convert_reduce_fusion.1
  2.3 0.6 add_maximum_fusion.last
  2.9 0.2 convert_reduce_fusion
  3.2 0.8 select_reduce_fusion
  4.0 0.1 slice_compare_fusion
  4.1 0.7 add_convert_fusion.keep
  4.7 0.0 copy-done
  4.7 154.1 %shard_map.85 = (f32[64,256]{1,0:T(8,128)}, f32[64,1024]{1,0:T(8,128)}, f32[64,256]{1,0:T(8,128)}) custom-call(s32[320]{0:T(512)} %copy-done, s32[320]{0:T(512)} %get-tuple-element.4.perm, f32[320]{0:T(512)} %add_convert_fusion.keep, s32[64]{0:T(128)} %add_maximum_fusion.last, f32[64]{0:T(128)} %convert_element_type.15.has, f32[64,256]{1,0:T(8,128)} %sol_ref.1, ...), custom_call_target="tpu_custom_call" | custom-call | tf_op jit(solution)/shard_map/pallas_call | solution.py:589
  158.8 1.5 copy.14
  160.3 1.7 %copy.15 = f32[64,1024]{1,0:T(8,128)} copy(f32[64,1024]{1,0:T(8,128)} %get-tuple-element.9) | data formatting | bytes 524288
  161.9 1.5 copy.16
  (1 shorter events, 0.0 us)
Async XLA Ops:
  1.6 3.1 %copy-start = (s32[320]{0:T(512)}, s32[320]{0:T(512)S(1)}, u32[]{:S(2)}) copy-start(s32[320]{0:T(512)S(1)} %reshape.32.gidx) | copy-start | bytes 3844

commit v2 on v1

v2 whole, which is shorter than its diff:
```python
import functools

import jax
import jax.numpy as jnp
from jax import lax
from jax.experimental import pallas as pl
from jax.experimental.pallas import tpu as pltpu
from jax.sharding import PartitionSpec as P

MESH = pl.DeviceIdType.MESH
F32, BF16 = jnp.float32, jnp.bfloat16
TB = 128
HOPS = 4
PIECES = 4
HIGH = lax.Precision.HIGHEST


def dot_high(left, right):
    return jnp.dot(left, right, precision=HIGH, preferred_element_type=F32)


def dot_lanes(left, right, precision=None):
    return lax.dot_general(
        left, right, (((1,), (1,)), ((), ())), precision=precision, preferred_element_type=F32
    )


def gram(value):
    return dot_lanes(value, value, HIGH)


def side_by_side(parts):
    return jnp.concatenate(parts, axis=1)


def inverses(matrices):
    size = matrices[0].shape[0]
    rows = lax.broadcasted_iota(jnp.int32, (size, 2 * size), 0)
    lanes = lax.broadcasted_iota(jnp.int32, (size, 2 * size), 1)
    eye = jnp.where(rows + size == lanes, 1.0, 0.0).astype(F32)[:, size:]

    def step(k, works):
        done = []
        for work in works:
            row = jnp.sum(jnp.where(rows == k, work, 0.0), axis=0, keepdims=True)
            col = jnp.sum(jnp.where(lanes == k, work, 0.0), axis=1, keepdims=True)
            pivot = jnp.sum(jnp.where(lanes[:1] == k, row, 0.0), axis=1, keepdims=True)
            row = row / pivot
            done.append(jnp.where(rows == k, row, work - col * row))
        return tuple(done)

    works = lax.fori_loop(0, size, step, tuple(side_by_side([a, eye]) for a in matrices))
    return [work[:, size:] for work in works]


def kernel(
    ny,
    slots,
    blocks_ref,
    counts_ref,
    sol_ref,
    res_ref,
    dir_ref,
    tiles_hbm,
    sol_out,
    res_out,
    dir_out,
    tiles,
    contrib,
    prefix,
    dirbuf,
    gbuf,
    rowsbuf,
    imgbuf,
    part,
    ringout,
    ringland,
    imgshare,
    xout,
    xland,
    sbuf,
    rland,
    gshare,
    hshare,
    dnext,
    ar_in,
    ar_sib,
    ar_x,
    ar_z,
    ar_out,
    keys_v,
    keys_s,
    table_v,
    table_s,
    table_sem,
    tile_sem,
    ring_send,
    ring_recv,
    agr_send,
    agr_recv,
    fwd_send,
    fwd_recv,
    x_send,
    x_recv,
    rs_send,
    rs_recv,
    ar_send,
    ar_recv,
):
    rows, cols = lax.axis_size("row"), lax.axis_size("col")
    chips = rows // 2
    nx = chips // ny
    r, z = lax.axis_index("row"), lax.axis_index("col")
    core, chip = lax.rem(r, 2), r // 2
    cx, cy = chip // ny, lax.rem(chip, ny)
    share = res_ref.shape[1] // TB
    width = share // PIECES
    blocks = 2 * rows
    hb = blocks // 2
    group = 2 * ny
    rhs = res_ref.shape[0]

    def at_col(d):
        return lax.rem(z + d + cols, cols)

    def ring_dev(d):
        return (r, at_col(1 if d == 0 else -1))

    sibling = (r + 1 - 2 * core, z)

    def chip_at(dx, dy):
        return lax.rem(cx + dx, nx) * ny + lax.rem(cy + dy, ny)

    offsets = [(dx, dy) for dx in range(nx) for dy in range(ny)]
    others = sorted(
        offsets[1:], key=lambda o: (-(min(o[0], nx - o[0]) + min(o[1], ny - o[1])), o)
    )

    def remote(src, dst, ss, rs, dev):
        return pltpu.make_async_remote_copy(
            src_ref=src, dst_ref=dst, send_sem=ss, recv_sem=rs, device_id=dev, device_id_type=MESH
        )

    per_chunk = share * slots
    chunk_copies = []
    for c in range(cols):
        chunk_copies.append(
            pltpu.make_async_copy(
                tiles_hbm.at[pl.ds(c * per_chunk, per_chunk)],
                tiles.at[pl.ds(c * per_chunk, per_chunk)],
                tile_sem.at[c],
            )
        )
        chunk_copies[-1].start()

    mine = core * hb + 2 * chip
    for j in range(2):
        dirbuf[mine + j] = dir_ref[:, j * TB : (j + 1) * TB].astype(BF16)
    dirbuf[blocks] = jnp.zeros((rhs, TB), BF16)
    gbuf[blocks] = jnp.zeros((rhs, TB), BF16)
    for i in range(share):
        rowsbuf[z * share + i] = res_ref[:, i * TB : (i + 1) * TB].astype(BF16)

    barrier = pltpu.get_barrier_semaphore()
    partners = [sibling]
    partners += [(chip_at(*o) * 2 + core, z) for o in others]
    partners += [(r, at_col(d)) for d in range(1, cols)]
    for dev in partners:
        pl.semaphore_signal(barrier, inc=1, device_id=dev, device_id_type=MESH)

    shape = blocks_ref.shape
    k = blocks_ref[...]
    place = (k // 4) * 2 + k % 2 + ((k // 2) % 2) * hb
    live = lax.broadcasted_iota(jnp.int32, shape, 1) < counts_ref[...]
    block_of = jnp.where(live, place, blocks)
    keys_v[...] = jnp.zeros_like(keys_v)
    table_v[...] = jnp.zeros_like(table_v)
    keys_v[:, :slots] = block_of
    copy_keys = pltpu.make_async_copy(keys_v, keys_s, table_sem.at[0])
    copy_keys.start()
    entry = lax.broadcasted_iota(jnp.int32, shape, 0) * slots + lax.broadcasted_iota(jnp.int32, shape, 1)
    key = block_of * (shape[0] * slots) + entry
    key_rows = jnp.transpose(
        jnp.concatenate([key, jnp.zeros((shape[0], TB - slots), jnp.int32)], axis=1)
    )
    lanes = lax.broadcasted_iota(jnp.int32, (shape[0], table_v.shape[1]), 1)
    found = [jnp.zeros((1, table_v.shape[1]), jnp.int32) for _ in range(5)]
    for s in range(slots):
        below = jnp.zeros((shape[0], shape[0]), jnp.int32)
        for other in range(slots):
            below = below + jnp.where(key_rows[other : other + 1] < key[:, s : s + 1], 1, 0)
        rank = jnp.sum(below, axis=1, keepdims=True)
        block_s = block_of[:, s : s + 1]
        for i, chosen in enumerate(
            (
                jnp.where(lanes == rank, entry[:, s : s + 1], 0),
                jnp.where(lanes == rank, block_s, 0),
                jnp.where(lanes == rank + 1, block_s + 1, 0),
                jnp.where(block_s <= lanes, 1, 0),
                jnp.where(block_s == lanes, 1, 0),
            )
        ):
            found[i] = found[i] + jnp.sum(chosen, axis=0, keepdims=True)
    order, at_place, before, upto, count = found
    table_v[0:1] = order
    table_v[1:2] = jnp.where(at_place + 1 == before, 1, 0)
    table_v[2:3] = jnp.maximum(upto - 1, 0)
    table_v[3:4] = jnp.where(count > 0, 1, 0)
    copy_table = pltpu.make_async_copy(table_v, table_s, table_sem.at[1])
    copy_table.start()
    pl.semaphore_wait(barrier, len(partners))

    def sensor_tiles(sensor):
        return side_by_side([tiles[sensor * slots + s] for s in range(slots)])

    def grad_piece(buf, shard, k):
        for i in range(width):
            sensor = shard * share + k * width + i
            value = jnp.dot(buf[sensor], sensor_tiles(sensor), preferred_element_type=F32)
            for s in range(slots):
                contrib[sensor * slots + s] = value[:, s * TB : (s + 1) * TB]

    def image_piece(buf, dest, d, k):
        for i in range(width):
            sensor = dest * share + k * width + i
            picked = side_by_side([buf[jnp.clip(keys_s[sensor, s], 0, blocks)] for s in range(slots)])
            part[d, k * width + i] = dot_lanes(picked, sensor_tiles(sensor))

    def sorted_sums():
        def one(j, run):
            run = run * table_s[1, j].astype(F32) + contrib[jnp.clip(table_s[0, j], 0, contrib.shape[0] - 1)]
            prefix[j] = run
            return run

        lax.fori_loop(0, contrib.shape[0], one, jnp.zeros((rhs, TB), F32), unroll=4)

    def block_sum(k):
        return prefix[jnp.clip(table_s[2, k], 0, prefix.shape[0] - 1)] * table_s[3, k].astype(F32)

    both_ways = [(k, d) for k in range(PIECES) for d in range(2)]

    def long_way(k):
        return 0 if k < PIECES // 2 else 1

    def col_at(d, steps):
        return at_col(steps if d == 0 else -steps)

    def gather_hop(buf, n, d, t, k, landed=False):
        back = t if landed else t - 1
        ref = buf.at[pl.ds(col_at(d, -back) * share + k * width, width)]
        return remote(ref, ref, ring_send.at[n, d, t - 1, k], ring_recv.at[n, d, t - 1, k], ring_dev(d))

    def gathers(d, t, k):
        return t < HOPS or (t == HOPS and long_way(k) == d)

    def gather_step(buf, n, t):
        got = []
        for k, d in both_ways:
            if gathers(d, t, k):
                gather_hop(buf, n, d, t, k, landed=True).wait_recv()
                if gathers(d, t + 1, k):
                    gather_hop(buf, n, d, t + 1, k).start()
                got.append((col_at(d, -t), k))
        return got

    def gather_sent(buf, n):
        for t in range(1, HOPS + 1):
            for k, d in both_ways:
                if gathers(d, t, k):
                    gather_hop(buf, n, d, t, k).wait_send()

    def ring_gather(buf, n):
        for k, d in both_ways:
            gather_hop(buf, n, d, 1, k).start()
        yield
        for k in range(PIECES):
            grad_piece(buf, z, k)
        yield
        for t in range(1, HOPS + 1):
            for shard, k in gather_step(buf, n, t):
                grad_piece(buf, shard, k)
            yield
        gather_sent(buf, n)

    def image_phase(it, buf):
        n_sum, n_all = 1 + 2 * it, 2 + 2 * it
        land, whole = ringland.at[it], imgbuf.at[it]

        def sums(d, t, k):
            return 1 < t <= HOPS or (t == 1 and long_way(k) == d)

        def hop(d, t, k):
            spot = pl.ds(k * width, width)
            return remote(
                ringout.at[d, t - 1, spot],
                land.at[d, t - 1, spot],
                ring_send.at[n_sum, d, t - 1, k],
                ring_recv.at[n_sum, d, t - 1, k],
                ring_dev(d),
            )

        def partial(d, t, k):
            image_piece(buf, col_at(d, HOPS + 1 - t), d, k)

        def send(d, t, k, arrived):
            if arrived:
                hop(d, t - 1, k).wait_recv()
            for i in range(k * width, (k + 1) * width):
                value = part[d, i]
                if arrived:
                    value = value + land[d, t - 2, i].astype(F32)
                ringout[d, t - 1, i] = value.astype(BF16)
            hop(d, t, k).start()

        for k, d in both_ways:
            t = 1 if sums(d, 1, k) else 2
            partial(d, t, k)
            send(d, t, k, False)
        for k, d in both_ways:
            if sums(d, 1, k):
                partial(d, 2, k)
        yield
        for t in range(2, HOPS + 1):
            for k, d in both_ways:
                if sums(d, t - 1, k):
                    send(d, t, k, True)
            if t < HOPS:
                for k, d in both_ways:
                    partial(d, t + 1, k)
            else:
                for k in range(PIECES):
                    image_piece(buf, z, 0, k)
            yield
        for k in range(PIECES):
            for d in range(2):
                hop(d, HOPS, k).wait_recv()
            for i in range(k * width, (k + 1) * width):
                total = part[0, i]
                for d in range(2):
                    total = total + land[d, HOPS - 1, i].astype(F32)
                if it:
                    total = total + imgshare[it, i]
                imgshare[it, i] = total
                whole[z * share + i] = total.astype(BF16)
            for d in range(2):
                gather_hop(whole, n_all, d, 1, k).start()
        yield
        for k in range(PIECES):
            grad_piece(whole, z, k)
        for t in range(1, HOPS + 1):
            for shard, k in gather_step(whole, n_all, t):
                grad_piece(whole, shard, k)
            yield
        for t in range(1, HOPS + 1):
            for k, d in both_ways:
                if sums(d, t, k):
                    hop(d, t, k).wait_send()
        gather_sent(whole, n_all)

    def plane(dx):
        return lax.rem(cx + dx, nx)

    def row_gather(buf, n):
        own = buf.at[pl.ds(mine, 2)]
        for dx, dy in others:
            remote(
                own,
                own,
                agr_send.at[n],
                agr_recv.at[n, (nx - dx) % nx],
                (chip_at(dx, dy) * 2 + core, z),
            ).start()

        def forward(dx, side):
            ref = buf.at[pl.ds(side * hb + plane(dx) * group, group)]
            return remote(ref, ref, fwd_send.at[n, dx], fwd_recv.at[n, dx], sibling)

        order = sorted(range(nx), key=lambda dx: min(dx, nx - dx))
        yield
        for dx in order:
            count = group if dx else group - 2
            ref = buf.at[pl.ds(core * hb, count)]
            if count:
                remote(ref, ref, agr_send.at[n], agr_recv.at[n, dx], sibling).wait_recv()
            forward(dx, core).start()
            yield
        for dx in order:
            forward(dx, 1 - core).wait_recv()
        yield
        for dx in order:
            forward(dx, core).wait_send()
        ref = buf.at[pl.ds(0, 2 * len(others))]
        remote(ref, ref, agr_send.at[n], agr_recv.at[n, 0], sibling).wait_send()

    def row_scatter(n, out):
        def swap(dx):
            spot = pl.ds(plane(dx) * group, group)
            return remote(xout.at[spot], xland.at[n, spot], x_send.at[n, dx], x_recv.at[n, dx], sibling)

        far_first = sorted(range(nx), key=lambda dx: (-min(dx, nx - dx), dx))

        for dx in far_first:
            start = plane(dx) * group
            for b in range(group):
                xout[start + b] = block_sum((1 - core) * hb + start + b).astype(BF16)
            swap(dx).start()
        slot = {o: i for i, o in enumerate(offsets[1:])}
        for dx in far_first:
            start = plane(dx) * group
            swap(dx).wait_recv()
            for b in range(group):
                total = block_sum(core * hb + start + b) + xland[n, start + b].astype(F32)
                sbuf[start + b] = total.astype(BF16)
            for o in others:
                if o[0] == dx:
                    remote(
                        sbuf.at[pl.ds(2 * chip_at(*o), 2)],
                        rland.at[n, pl.ds(2 * slot[o], 2)],
                        rs_send.at[n],
                        rs_recv.at[n],
                        (chip_at(*o) * 2 + core, z),
                    ).start()
        for j in range(2):
            out[j] = block_sum(mine + j) + xland[n, 2 * chip + j].astype(F32)
        yield
        every = rland.at[n]
        remote(every, every, rs_send.at[n], rs_recv.at[n], sibling).wait_recv()
        for j in range(2):
            total = out[j]
            for i in range(len(others)):
                total = total + rland[n, 2 * i + j].astype(F32)
            out[j] = total
        yield
        remote(every, every, rs_send.at[n], rs_recv.at[n], sibling).wait_send()
        for dx in far_first:
            swap(dx).wait_send()

    def all_sum(n, value):
        size = value.shape[0]
        part_rows = size // 2
        whole, own_half = pl.ds(0, size), pl.ds(core * part_rows, part_rows)
        half = pl.ds(0, part_rows)
        ar_in[n, whole] = value
        first = remote(
            ar_in.at[n, whole], ar_sib.at[n, whole], ar_send.at[n, 0], ar_recv.at[n, 0], sibling
        )
        first.start()
        yield
        first.wait_recv()
        ar_x[n, chip, half] = ar_in[n, own_half] + ar_sib[n, own_half]
        mine_x = ar_x.at[n, chip, half]
        for o in others:
            remote(
                mine_x, mine_x, ar_send.at[n, 1], ar_recv.at[n, 1], (chip_at(*o) * 2 + core, z)
            ).start()
        yield
        every_x = ar_x.at[n, pl.ds(0, len(others)), half]
        remote(every_x, every_x, ar_send.at[n, 1], ar_recv.at[n, 1], sibling).wait_recv()
        total = ar_x[n, 0, half]
        for i in range(1, chips):
            total = total + ar_x[n, i, half]
        ar_z[n, z, half] = total
        mine_z = ar_z.at[n, z, half]
        for d in range(1, cols):
            remote(mine_z, mine_z, ar_send.at[n, 2], ar_recv.at[n, 2], (r, at_col(d))).start()
        yield
        every_z = ar_z.at[n, pl.ds(0, cols - 1), half]
        remote(every_z, every_z, ar_send.at[n, 2], ar_recv.at[n, 2], sibling).wait_recv()
        total = ar_z[n, 0, half]
        for i in range(1, cols):
            total = total + ar_z[n, i, half]
        ar_out[n, own_half] = total
        mine_out = ar_out.at[n, own_half]
        final = remote(mine_out, mine_out, ar_send.at[n, 3], ar_recv.at[n, 3], sibling)
        final.start()
        yield
        final.wait_recv()
        yield
        first.wait_send()
        remote(every_x, every_x, ar_send.at[n, 1], ar_recv.at[n, 1], sibling).wait_send()
        remote(every_z, every_z, ar_send.at[n, 2], ar_recv.at[n, 2], sibling).wait_send()
        final.wait_send()

    def advance(gen, times=1):
        for _ in range(times):
            next(gen, None)

    def finish(gen):
        for _ in gen:
            pass

    def wide(ref):
        return side_by_side([ref[i] for i in range(ref.shape[0])])

    def to_blocks(value):
        return [value[:, i * TB : (i + 1) * TB] for i in range(value.shape[1] // TB)]

    def pair(left, right):
        return side_by_side([left, right])

    def folded(value):
        return pair(value[: rhs // 2], value[rhs // 2 :])

    def unfolded(value):
        return jnp.concatenate([value[:, :rhs], value[:, rhs:]], axis=0)

    resid = ring_gather(rowsbuf, 0)
    advance(resid)
    direct = row_gather(dirbuf, 0)
    advance(direct)
    for c in chunk_copies:
        c.wait()
    copy_keys.wait()
    copy_table.wait()
    advance(resid, 3)
    advance(direct, nx + 1)
    image = image_phase(0, dirbuf)
    advance(image)
    finish(resid)
    advance(image)
    sorted_sums()
    rowsc = row_scatter(0, gshare)
    advance(image)
    advance(rowsc)
    advance(image)
    finish(direct)
    advance(image)

    for it in range(2):
        advance(image)
        if it == 0:
            finish(rowsc)
            curv_gamma = pair(gram(wide(imgshare.at[0])), gram(wide(gshare)))
            summed = all_sum(0, curv_gamma)
        else:
            summed = all_sum(1, folded(gram(wide(imgshare.at[1]))))
        advance(summed)
        advance(image)
        advance(summed)
        advance(image)
        advance(summed)
        advance(image)
        sorted_sums()
        rowsc = row_scatter(1 + it, hshare)
        advance(rowsc)
        finish(summed)
        finish(image)
        if it == 0:
            both = ar_out[0]
            curvature, gamma = both[:, :rhs], both[:, rhs:]
        else:
            curvature = unfolded(ar_out[1, pl.ds(0, rhs // 2)])
        inv_curv, inv_gamma = inverses([curvature, gamma])
        alpha_t = dot_high(gamma, inv_curv)
        finish(rowsc)
        step_g = to_blocks(dot_high(alpha_t, wide(hshare)))
        for j in range(2):
            gshare[j] = gshare[j] - step_g[j]
            if it == 0:
                gbuf[mine + j] = gshare[j].astype(BF16)
        if it == 0:
            direct = row_gather(gbuf, 1)
            advance(direct)
        summed = all_sum(2 + it, folded(gram(wide(gshare))))
        advance(summed)
        old_dir = dir_ref[...] if it == 0 else wide(dnext)
        old_sol = sol_ref[...] if it == 0 else sol_out[...]
        old_res = res_ref[...] if it == 0 else res_out[...]
        sol_out[...] = old_sol + dot_high(alpha_t, old_dir)
        advance(summed)
        res_out[...] = old_res - dot_high(alpha_t, wide(imgshare.at[it]))
        if it == 0:
            advance(direct, nx + 1)
            image = image_phase(1, gbuf)
            advance(image)
            advance(summed)
            advance(image)
            advance(summed)
            advance(image)
        finish(summed)
        gamma_next = unfolded(ar_out[2 + it, pl.ds(0, rhs // 2)])
        beta_t = dot_high(gamma_next, inv_gamma)
        step_d = dot_high(beta_t, old_dir)
        if it == 0:
            for i, value in enumerate(to_blocks(dot_high(beta_t, wide(imgshare.at[0])))):
                imgshare[1, i] = value
            advance(image)
            for j, value in enumerate(to_blocks(step_d)):
                dnext[j] = gshare[j] + value
            finish(direct)
            advance(image)
        else:
            dir_out[...] = wide(gshare) + step_d
        gamma = gamma_next


def hand_over(*refs):
    for source, target in zip(refs[:3], refs[3:]):
        target[...] = source[...]


def per_device(solution, residual, direction, jacobian_tiles, tile_blocks, tile_counts):
    rows, cols = lax.axis_size("row"), lax.axis_size("col")
    chips = rows // 2
    ny = 4 if chips % 4 == 0 else chips
    nx = chips // ny
    rhs = residual.shape[0]
    sensors, slots = tile_blocks.shape
    entries = sensors * slots
    blocks = 2 * rows
    share = residual.shape[1] // TB
    tile = (rhs, TB)
    vmem = pl.BlockSpec(memory_space=pltpu.VMEM)
    dma = pltpu.SemaphoreType.DMA
    results = pl.pallas_call(
        functools.partial(kernel, ny, slots),
        out_shape=[
            jax.ShapeDtypeStruct(solution.shape, F32),
            jax.ShapeDtypeStruct(residual.shape, F32),
            jax.ShapeDtypeStruct(direction.shape, F32),
        ],
        in_specs=[vmem] * 5 + [pl.BlockSpec(memory_space=pl.ANY)],
        out_specs=[vmem] * 3,
        scratch_shapes=[
            pltpu.VMEM((entries, TB, TB), BF16),
            pltpu.VMEM((entries, *tile), F32),
            pltpu.VMEM((entries, *tile), F32),
            pltpu.VMEM((blocks + 1, *tile), BF16),
            pltpu.VMEM((blocks + 1, *tile), BF16),
            pltpu.VMEM((sensors, *tile), BF16),
            pltpu.VMEM((2, sensors, *tile), BF16),
            pltpu.VMEM((2, share, *tile), F32),
            pltpu.VMEM((2, HOPS, share, *tile), BF16),
            pltpu.VMEM((2, 2, HOPS, share, *tile), BF16),
            pltpu.VMEM((2, share, *tile), F32),
            pltpu.VMEM((blocks // 2, *tile), BF16),
            pltpu.VMEM((3, blocks // 2, *tile), BF16),
            pltpu.VMEM((blocks // 2, *tile), BF16),
            pltpu.VMEM((3, 2 * (chips - 1), *tile), BF16),
            pltpu.VMEM((2, *tile), F32),
            pltpu.VMEM((2, *tile), F32),
            pltpu.VMEM((2, *tile), F32),
            pltpu.VMEM((4, rhs, TB), F32),
            pltpu.VMEM((4, rhs, TB), F32),
            pltpu.VMEM((4, chips, rhs // 2, TB), F32),
            pltpu.VMEM((4, cols, rhs // 2, TB), F32),
            pltpu.VMEM((4, rhs, TB), F32),
            pltpu.VMEM((sensors, TB), jnp.int32),
            pltpu.SMEM((sensors, TB), jnp.int32),
            pltpu.VMEM((8, -(-entries // TB) * TB), jnp.int32),
            pltpu.SMEM((8, -(-entries // TB) * TB), jnp.int32),
            dma((2,)),
            dma((cols,)),
            dma((5, 2, HOPS, PIECES)),
            dma((5, 2, HOPS, PIECES)),
            dma((2,)),
            dma((2, nx)),
            dma((2, nx)),
            dma((2, nx)),
            dma((3, nx)),
            dma((3, nx)),
            dma((3,)),
            dma((3,)),
            dma((4, 4)),
            dma((4, 4)),
        ],
        compiler_params=pltpu.CompilerParams(
            collective_id=0, has_side_effects=True, vmem_limit_bytes=58 * 1024 * 1024
        ),
    )(tile_blocks, tile_counts, solution, residual, direction, jacobian_tiles.reshape(entries, TB, TB))
    return pl.pallas_call(
        hand_over,
        out_shape=[jax.ShapeDtypeStruct(v.shape, F32) for v in results],
        in_specs=[vmem] * 3,
        out_specs=[vmem] * 3,
    )(*results)


def solution(mesh):
    both = P(None, ("row", "col"))
    return jax.shard_map(
        per_device,
        mesh=mesh,
        in_specs=(both, both, both, P("row", "col", None, None), P("row", "col"), P("row", "col")),
        out_specs=(both, both, both),
        check_vma=False,
    )
```

time: 164 us -> 147 us (0.90)
  Pallas kernels: 154 us -> 143 us
  other arithmetic: 3.83 us -> 0 us
  local copies, waits for them, and re-layouts: 4.86 us -> 2.75 us
    pallas_call x1, Pallas kernels: 154 us -> 141 us  [per_device(): pl.pallas_call(functools.partial(kernel, ny, slots), out_shape=[jax.Shape...]
    unnamed x5 -> x2, local copies, waits for them, and re-layouts: 4.62 us -> 2.75 us
    pallas_call x0 -> x1, Pallas kernels: none -> 1.71 us  [per_device(): pl.pallas_call(hand_over, out_shape=[jax.ShapeDtypeStruct(v.shape, F32) f...]
where the time goes in v2:
time: 147 us; the launch traced here: 146 us
  Pallas kernels  143 us (97%)
  local copies, waits for them, and re-layouts  2.75 us (2%)
    pallas_call x1, Pallas kernels, per_device(): pl.pallas_call(functools.partial(kernel, ny, slots), out_shape=[jax.Shape...  141 us

profile of v2, /device:TPU:1, one launch (start us, length us, event | category | flops | bytes accessed | tf_op | source)
XLA Modules:
  0.0 146.4 jit_solution(14035118065240674673)
XLA Ops:
  0.6 1.4 copy.9.blocks_ref
  2.0 1.4 copy.10.counts_ref
  3.4 141.3 %shard_map.85 = (f32[64,256]{1,0:T(8,128)}, f32[64,1024]{1,0:T(8,128)}, f32[64,256]{1,0:T(8,128)}) custom-call(s32[64,5]{1,0:T(8,128)} %copy.9.blocks_ref, s32[64,1]{1,0:T(8,128)} %copy.10.counts_ref, f32[64,256]{1,0:T(8,128)} %sol_ref.1, f32[64,1024]{1,0:T(8,128)} %res_ref.1, f32[64,256]{1,0:T(8,128)} %dir_ref.1, bf16[320,128,128]{2,1,0:T(8,128)(2,1)} %bitcast.1), custom_call_target="tpu_custom_call" | custom-call | tf_op jit(solution)/shard_map/pallas_call | solution.py:615
  144.7 1.7 %shard_map.86 = (f32[64,256]{1,0:T(8,128)}, f32[64,1024]{1,0:T(8,128)}, f32[64,256]{1,0:T(8,128)}) custom-call(f32[64,256]{1,0:T(8,128)} %get-tuple-element.6.refs_0_, f32[64,1024]{1,0:T(8,128)} %get-tuple-element.7.refs_1_, f32[64,256]{1,0:T(8,128)} %get-tuple-element.8.refs_2_), custom_call_target="tpu_custom_call" | custom-call | tf_op jit(solution)/shard_map/pallas_call | solution.py:671

commit v3 on v2

--- a/solution.py
+++ b/solution.py
@@ -168,13 +168,16 @@
     for dev in partners:
         pl.semaphore_signal(barrier, inc=1, device_id=dev, device_id_type=MESH)
 
-    shape = blocks_ref.shape
-    k = blocks_ref[...]
-    place = (k // 4) * 2 + k % 2 + ((k // 2) % 2) * hb
-    live = lax.broadcasted_iota(jnp.int32, shape, 1) < counts_ref[...]
-    block_of = jnp.where(live, place, blocks)
+    shape = (blocks_ref.shape[1], slots)
     keys_v[...] = jnp.zeros_like(keys_v)
     table_v[...] = jnp.zeros_like(table_v)
+    table_v[:slots, : shape[0]] = blocks_ref[...]
+    table_v[slots : slots + 1, : shape[0]] = counts_ref[...]
+    by_sensor = jnp.transpose(table_v[:, :TB])[: shape[0]]
+    k = by_sensor[:, :slots]
+    place = (k // 4) * 2 + k % 2 + ((k // 2) % 2) * hb
+    live = lax.broadcasted_iota(jnp.int32, shape, 1) < by_sensor[:, slots : slots + 1]
+    block_of = jnp.where(live, place, blocks)
     keys_v[:, :slots] = block_of
     copy_keys = pltpu.make_async_copy(keys_v, keys_s, table_sem.at[0])
     copy_keys.start()
@@ -552,7 +555,7 @@
             curvature = unfolded(ar_out[1, pl.ds(0, rhs // 2)])
         inv_curv, inv_gamma = inverses([curvature, gamma])
         alpha_t = dot_high(gamma, inv_curv)
-        finish(rowsc)
+        advance(rowsc)
         step_g = to_blocks(dot_high(alpha_t, wide(hshare)))
         for j in range(2):
             gshare[j] = gshare[j] - step_g[j]
@@ -563,6 +566,7 @@
             advance(direct)
         summed = all_sum(2 + it, folded(gram(wide(gshare))))
         advance(summed)
+        finish(rowsc)
         old_dir = dir_ref[...] if it == 0 else wide(dnext)
         old_sol = sol_ref[...] if it == 0 else sol_out[...]
         old_res = res_ref[...] if it == 0 else res_out[...]
@@ -577,7 +581,7 @@
             advance(image)
             advance(summed)
             advance(image)
-        finish(summed)
+        advance(summed, 3)
         gamma_next = unfolded(ar_out[2 + it, pl.ds(0, rhs // 2)])
         beta_t = dot_high(gamma_next, inv_gamma)
         step_d = dot_high(beta_t, old_dir)
@@ -591,6 +595,7 @@
             advance(image)
         else:
             dir_out[...] = wide(gshare) + step_d
+        finish(summed)
         gamma = gamma_next
 
 
@@ -667,7 +672,7 @@
         compiler_params=pltpu.CompilerParams(
             collective_id=0, has_side_effects=True, vmem_limit_bytes=58 * 1024 * 1024
         ),
-    )(tile_blocks, tile_counts, solution, residual, direction, jacobian_tiles.reshape(entries, TB, TB))
+    )(tile_blocks.T, tile_counts.T, solution, residual, direction, jacobian_tiles.reshape(entries, TB, TB))
     return pl.pallas_call(
         hand_over,
         out_shape=[jax.ShapeDtypeStruct(v.shape, F32) for v in results],

time: 147 us -> 144 us (0.980)
  local copies, waits for them, and re-layouts: 2.75 us -> 0 us
    unnamed x2 -> x0, local copies, waits for them, and re-layouts: 2.75 us -> none
where the time goes in v3:
time: 144 us
  Pallas kernels  143 us (99%)
    pallas_call x1, Pallas kernels, per_device(): pl.pallas_call(functools.partial(kernel, ny, slots), out_shape=[jax.Shape...  141 us

profile of v3, /device:TPU:1, one launch (start us, length us, event | category | flops | bytes accessed | tf_op | source)
XLA Modules:
  0.0 143.8 jit_solution(12441339117920295158)
XLA Ops:
  0.6 141.5 %shard_map.85 = (f32[64,256]{1,0:T(8,128)}, f32[64,1024]{1,0:T(8,128)}, f32[64,256]{1,0:T(8,128)}) custom-call(s32[5,64]{1,0:T(8,128)} %bitcast.4, s32[1,64]{1,0:T(1,128)} %bitcast.5, f32[64,256]{1,0:T(8,128)} %sol_ref.1, f32[64,1024]{1,0:T(8,128)} %res_ref.1, f32[64,256]{1,0:T(8,128)} %dir_ref.1, bf16[320,128,128]{2,1,0:T(8,128)(2,1)} %bitcast.3), custom_call_target="tpu_custom_call" | custom-call | tf_op jit(solution)/shard_map/pallas_call | solution.py:620
  142.1 1.7 %shard_map.86 = (f32[64,256]{1,0:T(8,128)}, f32[64,1024]{1,0:T(8,128)}, f32[64,256]{1,0:T(8,128)}) custom-call(f32[64,256]{1,0:T(8,128)} %get-tuple-element.6.refs_0_, f32[64,1024]{1,0:T(8,128)} %get-tuple-element.7.refs_1_, f32[64,256]{1,0:T(8,128)} %get-tuple-element.8.refs_2_), custom_call_target="tpu_custom_call" | custom-call | tf_op jit(solution)/shard_map/pallas_call | solution.py:676
